TPU v7x, 1024 devices: a whole 4x4x32 slice. The times are simulated.
1024 devices in a mesh: expert: 64 (over x, z_lo), fsdp: 16 (over y, z_hi, core).
Axes of the slice: x: 4, y: 4, z: 32 (z_hi: 2, z_lo: 16; z = z_hi * 16 + z_lo), core: 2. Of those that a mesh axis runs over, the one named last changes fastest.
Arguments:
- tokens: bfloat16 [1536, 5120], P('expert', 'fsdp'), may hold values from -6 to 6
- route: int32 [1536, 1], P('expert'), may hold values from 0 to 3; in each aligned block of 24 rows (0 to 23, 24 to 47, ...) at most 8 rows name the same one
- score: bfloat16 [1536], P('expert'), may hold values from 0.099609375 to 1
- grad_out: bfloat16 [1536, 5120], P('expert', 'fsdp'), may hold values from -1.1953125 to 1.1953125
- w_gate: bfloat16 [5120, 32768], P('fsdp', 'expert'), may hold values from -0.078125 to 0.078125
- w_up: bfloat16 [5120, 32768], P('fsdp', 'expert'), may hold values from -0.078125 to 0.078125
- w_down: bfloat16 [32768, 5120], P('expert', 'fsdp'), may hold values from -0.0625 to 0.0625
Outputs:
- grad_tokens: bfloat16 [1536, 5120], P('expert', 'fsdp')
- grad_score: float32 [1536], P('expert')
- grad_gate: bfloat16 [5120, 32768], P('fsdp', 'expert')
- grad_up: bfloat16 [5120, 32768], P('fsdp', 'expert')
- grad_down: bfloat16 [32768, 5120], P('expert', 'fsdp')
Inputs may be any that keep to these rules, and one draw needn't show every extreme that they name: `route`: among the 24 tokens of each block, no expert is named more than 8 times; some block names some expert exactly 8 times.
All inputs are finite; a program needn't handle non-finite values.
Results may differ from a plain program's by a relative error of at most 0.0095.
Values may be sent and summed in bfloat16 or wider, within the bound.
A program may use at most 32 MiB of HBM per device.

v0:
```python
import jax
import jax.numpy as jnp
from jax import lax
from jax.sharding import PartitionSpec as P

EXPERTS = 4
MOST = 8


def activate(gate_vals, up_vals, back_vals, slot_scale):
    sigmoid_gate = jax.nn.sigmoid(gate_vals)
    silu_gate = gate_vals * sigmoid_gate
    hidden_vals = silu_gate * up_vals
    scaled_hidden = (slot_scale[:, None] * hidden_vals).astype(jnp.bfloat16)
    proj_grad = slot_scale[:, None] * back_vals
    gate_grad = (
        proj_grad * up_vals * sigmoid_gate * (1.0 + gate_vals * (1.0 - sigmoid_gate))
    ).astype(jnp.bfloat16)
    up_grad = (proj_grad * silu_gate).astype(jnp.bfloat16)
    score_terms = jnp.sum(hidden_vals * back_vals, axis=-1)
    return (scaled_hidden, gate_grad, up_grad, score_terms)


def per_device(tokens, route, score, grad_out, w_gate, w_up, w_down):
    expert_count = lax.axis_size("expert")
    fsdp_count = lax.axis_size("fsdp")
    shard_count = expert_count // EXPERTS
    feature_cols = tokens.shape[1]
    hidden_cols = w_gate.shape[1]
    slot_rows = expert_count * MOST
    expert_ids = jnp.arange(EXPERTS, dtype=jnp.int32)
    onehot = (route == expert_ids[None, :]).astype(jnp.int32)
    ranks_local = jnp.cumsum(onehot, axis=0) - 1
    slot_ids = jnp.arange(MOST, dtype=jnp.int32)
    placement = (
        (onehot[:, :, None] == 1) & (ranks_local[:, :, None] == slot_ids[None, None, :])
    ).astype(jnp.bfloat16)
    packed_tokens = jnp.einsum(
        "tem,td->emd", placement, tokens, preferred_element_type=jnp.float32
    ).astype(jnp.bfloat16)
    packed_grads = jnp.einsum(
        "tem,td->emd", placement, grad_out, preferred_element_type=jnp.float32
    ).astype(jnp.bfloat16)
    packed_scores = jnp.einsum(
        "tem,t->em", placement, score, preferred_element_type=jnp.float32
    ).astype(jnp.bfloat16)
    slot_tokens, slot_grads, slot_scores = (
        lax.all_to_all(
            jnp.repeat(packed_tokens, shard_count, axis=0),
            "expert",
            split_axis=0,
            concat_axis=0,
            tiled=True,
        ),
        lax.all_to_all(
            jnp.repeat(packed_grads, shard_count, axis=0),
            "expert",
            split_axis=0,
            concat_axis=0,
            tiled=True,
        ),
        lax.all_to_all(
            jnp.repeat(packed_scores, shard_count, axis=0),
            "expert",
            split_axis=0,
            concat_axis=0,
            tiled=True,
        ),
    )
    slot_tokens = slot_tokens.reshape(slot_rows, feature_cols)
    slot_grads = slot_grads.reshape(slot_rows, feature_cols)
    slot_scale = slot_scores.reshape(slot_rows).astype(jnp.float32)
    weight_pair = jnp.concatenate([w_gate, w_up], axis=1)
    share_rows = slot_rows // fsdp_count
    forward = jnp.dot(slot_tokens, weight_pair, preferred_element_type=jnp.float32)
    backward = lax.dot_general(
        slot_grads, w_down, (((1,), (1,)), ((), ())), preferred_element_type=jnp.float32
    )
    summed = lax.psum_scatter(
        jnp.concatenate([forward, backward], axis=1), "fsdp", scatter_dimension=0, tiled=True
    )
    first_share = lax.axis_index("fsdp") * share_rows
    share_scale = lax.dynamic_slice_in_dim(slot_scale, first_share, share_rows, 0)
    scaled_hidden, gate_grad, up_grad, score_terms = activate(
        summed[:, :hidden_cols],
        summed[:, hidden_cols : 2 * hidden_cols],
        summed[:, 2 * hidden_cols :],
        share_scale,
    )
    activations = jnp.concatenate([scaled_hidden, gate_grad, up_grad], axis=1)
    activations, score_piece = (
        lax.all_gather(activations, "fsdp", axis=0, tiled=True),
        lax.all_gather(score_terms.astype(jnp.bfloat16), "fsdp", axis=0, tiled=True),
    )
    scaled_hidden = activations[:, :hidden_cols]
    gate_grad = activations[:, hidden_cols : 2 * hidden_cols]
    up_grad = activations[:, 2 * hidden_cols :]
    contract_rows = (((0,), (0,)), ((), ()))
    grad_gate = lax.dot_general(
        slot_tokens, gate_grad, contract_rows, preferred_element_type=jnp.float32
    ).astype(jnp.bfloat16)
    grad_up = lax.dot_general(
        slot_tokens, up_grad, contract_rows, preferred_element_type=jnp.float32
    ).astype(jnp.bfloat16)
    grad_down = lax.dot_general(
        scaled_hidden, slot_grads, contract_rows, preferred_element_type=jnp.float32
    ).astype(jnp.bfloat16)
    contract_cols = (((1,), (1,)), ((), ()))
    token_piece = lax.dot_general(
        gate_grad, w_gate, contract_cols, preferred_element_type=jnp.float32
    )
    token_piece = token_piece + lax.dot_general(
        up_grad, w_up, contract_cols, preferred_element_type=jnp.float32
    )
    token_piece = token_piece.astype(jnp.bfloat16).reshape(expert_count, MOST, feature_cols)
    returned_grads, returned_scores = (
        lax.all_to_all(token_piece, "expert", split_axis=0, concat_axis=0, tiled=True),
        lax.all_to_all(
            score_piece.reshape(expert_count, MOST),
            "expert",
            split_axis=0,
            concat_axis=0,
            tiled=True,
        ),
    )
    grads_summed = (
        returned_grads.reshape(EXPERTS, shard_count, MOST, feature_cols).astype(jnp.float32).sum(1)
    )
    scores_summed = returned_scores.reshape(EXPERTS, shard_count, MOST).astype(jnp.float32).sum(1)
    placement_wide = placement.astype(jnp.float32)
    grad_tokens = jnp.einsum("tem,emd->td", placement_wide, grads_summed).astype(jnp.bfloat16)
    grad_score = jnp.einsum("tem,em->t", placement_wide, scores_summed)
    return (grad_tokens, grad_score, grad_gate, grad_up, grad_down)


def solution(mesh):
    return jax.shard_map(
        per_device,
        mesh=mesh,
        in_specs=(
            P("expert", "fsdp"),
            P("expert", None),
            P("expert"),
            P("expert", "fsdp"),
            P("fsdp", "expert"),
            P("fsdp", "expert"),
            P("expert", "fsdp"),
        ),
        out_specs=(
            P("expert", "fsdp"),
            P("expert"),
            P("fsdp", "expert"),
            P("fsdp", "expert"),
            P("expert", "fsdp"),
        ),
        check_vma=False,
    )
```

profile of v0, /device:TPU:6, one launch (start us, length us, event | category | flops | bytes accessed | tf_op | source)
XLA Modules:
  0.0 561.4 jit_solution(9499986834457079672)
XLA Ops:
  8.2 0.9 convolution_convert_fusion.3
  9.8 29.5 %all-to-all-start.2 = ((bf16[64,8,320]{2,1,0:T(8,128)(2,1)}), bf16[64,8,320]{2,1,0:T(8,128)(2,1)S(1)}, u32[]{:S(2)}, u32[]{:S(2)}) async-start(bf16[64,8,320]{2,1,0:T(8,128)(2,1)} %bitcast.7), calls=%async_computation.2 | async-start | bytes 786432 | tf_op jit(solution)/shard_map/all_to_all | solution.py:55
  39.3 0.9 convolution_convert_fusion.4
  40.3 42.9 %all-to-all-done.2 = bf16[64,8,320]{2,1,0:T(8,128)(2,1)S(1)} async-done(((bf16[64,8,320]{2,1,0:T(8,128)(2,1)}), bf16[64,8,320]{2,1,0:T(8,128)(2,1)S(1)}, u32[]{:S(2)}, u32[]{:S(2)}) %all-to-all-start.2) | async-done | bytes 327712 | tf_op jit(solution)/shard_map/all_to_all | solution.py:55
  84.0 13.6 %all-to-all-start.1 = ((bf16[64,8,320]{2,1,0:T(8,128)(2,1)}), bf16[64,8,320]{2,1,0:T(8,128)(2,1)S(1)}, u32[]{:S(2)}, u32[]{:S(2)}) async-start(bf16[64,8,320]{2,1,0:T(8,128)(2,1)} %bitcast.4), calls=%async_computation.1 | async-start | bytes 786432 | tf_op jit(solution)/shard_map/all_to_all | solution.py:48
  98.0 43.3 %all-to-all-done.1 = bf16[64,8,320]{2,1,0:T(8,128)(2,1)S(1)} async-done(((bf16[64,8,320]{2,1,0:T(8,128)(2,1)}), bf16[64,8,320]{2,1,0:T(8,128)(2,1)S(1)}, u32[]{:S(2)}, u32[]{:S(2)}) %all-to-all-start.1) | async-done | bytes 327712 | tf_op jit(solution)/shard_map/all_to_all | solution.py:48
  142.0 1.9 pad_maximum_fusion
  145.7 13.6 %all-to-all-start = ((bf16[64,1,8]{2,1,0:T(2,128)(2,1)}), bf16[64,1,8]{2,1,0:T(2,128)(2,1)S(1)}, u32[]{:S(2)}, u32[]{:S(2)}) async-start(bf16[64,1,8]{2,1,0:T(2,128)(2,1)} %copy.26), calls=%async_computation | async-start | bytes 65536 | tf_op jit(solution)/shard_map/all_to_all | solution.py:62
  159.4 20.0 %all-to-all-done = bf16[64,1,8]{2,1,0:T(2,128)(2,1)S(1)} async-done(((bf16[64,1,8]{2,1,0:T(2,128)(2,1)}), bf16[64,1,8]{2,1,0:T(2,128)(2,1)S(1)}, u32[]{:S(2)}, u32[]{:S(2)}) %all-to-all-start) | async-done | bytes 1056 | tf_op jit(solution)/shard_map/all_to_all | solution.py:62
  179.6 177.1 %reduce-scatter.2.cloned.1.call-done = f32[32,1536]{1,0:T(8,128)} async-done(((f32[512,1536]{1,0:T(8,128)}), f32[32,1536]{1,0:T(8,128)}) %reduce-scatter.2.cloned.1.call-update) | async-done | bytes 196624 | tf_op jit(solution)/shard_map/reduce_scatter | solution.py:79
  356.7 1.1 multiply_convert_fusion.2
  358.5 1.3 dynamic-slice
  360.6 112.4 %all-reduce = bf16[512]{0:T(512)(128)(2,1)S(1)} all-reduce(bf16[512]{0:T(512)(128)(2,1)S(1)} %dynamic-update-slice), channel_id=1, replica_groups=mesh['expert'=64,'fsdp'=16] {'fsdp'}, use_global_device_ids=true, to_apply=%add | all-reduce | flops 512 | bytes 2048
  473.8 19.2 %all-to-all-start.4 = ((bf16[64,1,8]{2,1,0:T(2,128)(2,1)}), bf16[64,1,8]{2,1,0:T(2,128)(2,1)S(1)}, u32[]{:S(2)}, u32[]{:S(2)}) async-start(bf16[64,1,8]{2,1,0:T(2,128)(2,1)} %all_to_all.28), calls=%async_computation.5 | async-start | bytes 65536 | tf_op jit(solution)/shard_map/all_to_all | solution.py:118
  493.1 1.4 fusion.10
  494.5 1.5 fusion
  496.0 0.9 copy.28
  497.0 16.1 %all-to-all-done.4 = bf16[64,1,8]{2,1,0:T(2,128)(2,1)S(1)} async-done(((bf16[64,1,8]{2,1,0:T(2,128)(2,1)}), bf16[64,1,8]{2,1,0:T(2,128)(2,1)S(1)}, u32[]{:S(2)}, u32[]{:S(2)}) %all-to-all-start.4) | async-done | bytes 1056 | tf_op jit(solution)/shard_map/all_to_all | solution.py:118
  513.1 6.6 %all-to-all-start.3 = ((bf16[64,8,320]{2,1,0:T(8,128)(2,1)}), bf16[64,8,320]{2,1,0:T(8,128)(2,1)S(1)}, u32[]{:S(2)}, u32[]{:S(2)}) async-start(bf16[64,8,320]{2,1,0:T(8,128)(2,1)} %bitcast.9), calls=%async_computation.4 | async-start | bytes 786432 | tf_op jit(solution)/shard_map/all_to_all | solution.py:117
  520.4 1.1 convolution_convert_fusion
  521.6 1.1 convolution_convert_fusion.1
  522.6 1.1 convolution_convert_fusion.2
  523.7 30.0 %all-to-all-done.3 = bf16[64,8,320]{2,1,0:T(8,128)(2,1)S(1)} async-done(((bf16[64,8,320]{2,1,0:T(8,128)(2,1)}), bf16[64,8,320]{2,1,0:T(8,128)(2,1)S(1)}, u32[]{:S(2)}, u32[]{:S(2)}) %all-to-all-start.3) | async-done | bytes 327712 | tf_op jit(solution)/shard_map/all_to_all | solution.py:117
  553.8 0.8 fusion.1
  (40 shorter events, 8.4 us)
Async XLA Ops:
  7.2 90.4 %copy-start = (bf16[512,320]{0,1:T(8,128)(2,1)S(1)}, bf16[512,320]{0,1:T(8,128)(2,1)}, u32[]{:S(2)}) copy-start(bf16[512,320]{0,1:T(8,128)(2,1)} %param.13) | copy-start | bytes 983044
  9.8 73.4 %all-to-all-start.2 = ((bf16[64,8,320]{2,1,0:T(8,128)(2,1)}), bf16[64,8,320]{2,1,0:T(8,128)(2,1)S(1)}, u32[]{:S(2)}, u32[]{:S(2)}) async-start(bf16[64,8,320]{2,1,0:T(8,128)(2,1)} %bitcast.7), calls=%async_computation.2 | async-start | bytes 786432 | tf_op jit(solution)/shard_map/all_to_all | solution.py:55
  39.3 102.0 %copy-start.1 = (bf16[320,512]{1,0:T(8,128)(2,1)S(1)}, bf16[320,512]{1,0:T(8,128)(2,1)}, u32[]{:S(2)}) copy-start(bf16[320,512]{1,0:T(8,128)(2,1)} %param.12) | copy-start | bytes 983044
  39.3 102.0 %copy-start.2 = (bf16[320,512]{1,0:T(8,128)(2,1)S(1)}, bf16[320,512]{1,0:T(8,128)(2,1)}, u32[]{:S(2)}) copy-start(bf16[320,512]{1,0:T(8,128)(2,1)} %param.11) | copy-start | bytes 983044
  84.0 57.3 %all-to-all-start.1 = ((bf16[64,8,320]{2,1,0:T(8,128)(2,1)}), bf16[64,8,320]{2,1,0:T(8,128)(2,1)S(1)}, u32[]{:S(2)}, u32[]{:S(2)}) async-start(bf16[64,8,320]{2,1,0:T(8,128)(2,1)} %bitcast.4), calls=%async_computation.1 | async-start | bytes 786432 | tf_op jit(solution)/shard_map/all_to_all | solution.py:48
  97.6 259.1 %reduce-scatter.2.cloned.1.call-start = ((), (), s32[]{:S(2)}) async-start(), calls=%async_computation.6 | async-start | bytes 3342336 | tf_op jit(solution)/shard_map/reduce_scatter | solution.py:79
  143.9 0.7 copy-start.4
  145.7 33.6 %all-to-all-start = ((bf16[64,1,8]{2,1,0:T(2,128)(2,1)}), bf16[64,1,8]{2,1,0:T(2,128)(2,1)S(1)}, u32[]{:S(2)}, u32[]{:S(2)}) async-start(bf16[64,1,8]{2,1,0:T(2,128)(2,1)} %copy.26), calls=%async_computation | async-start | bytes 65536 | tf_op jit(solution)/shard_map/all_to_all | solution.py:62
  159.3 333.8 %all-gather.2.cloned.1.call-start = ((), (), s32[]{:S(2)}) async-start(), calls=%async_computation.7 | async-start | bytes 1671168 | tf_op jit(solution)/shard_map/all_gather | solution.py:92
  473.8 39.3 %all-to-all-start.4 = ((bf16[64,1,8]{2,1,0:T(2,128)(2,1)}), bf16[64,1,8]{2,1,0:T(2,128)(2,1)S(1)}, u32[]{:S(2)}, u32[]{:S(2)}) async-start(bf16[64,1,8]{2,1,0:T(2,128)(2,1)} %all_to_all.28), calls=%async_computation.5 | async-start | bytes 65536 | tf_op jit(solution)/shard_map/all_to_all | solution.py:118
  494.5 25.9 %copy-start.3 = (bf16[512,1536]{1,0:T(8,128)(2,1)S(1)}, bf16[512,1536]{1,0:T(8,128)(2,1)}, u32[]{:S(2)}) copy-start(bf16[512,1536]{1,0:T(8,128)(2,1)} %all-gather.2.cloned.1.call-done) | copy-start | bytes 4718596
  513.1 40.6 %all-to-all-start.3 = ((bf16[64,8,320]{2,1,0:T(8,128)(2,1)}), bf16[64,8,320]{2,1,0:T(8,128)(2,1)S(1)}, u32[]{:S(2)}, u32[]{:S(2)}) async-start(bf16[64,8,320]{2,1,0:T(8,128)(2,1)} %bitcast.9), calls=%async_computation.4 | async-start | bytes 786432 | tf_op jit(solution)/shard_map/all_to_all | solution.py:117
Sparse Core Ops, SparseCore 0:
  144.1 212.5 reduce-scatter.1
  361.7 119.1 all-gather.1
where the time goes:
time: 562 us; the launch traced here: 561 us
  waiting for transfers between devices  329 us (59%)
  blocking collectives  112 us (20%)
  starting transfers between devices  82.5 us (15%)
  between operations  14.9 us (3%)
  matrix products  10.7 us (2%)
  local copies, waits for them, and re-layouts  6.78 us (1%)
    reduce_scatter x1, waiting for transfers between devices, per_device(): lax.psum_scatter(jnp.concatenate([forward, backward], axis=1), 'fsdp', sc...  177 us
    unnamed x1, blocking collectives  112 us
    all_to_all x1, waiting for transfers between devices, per_device(): lax.all_to_all(jnp.repeat(packed_tokens, shard_count, axis=0), 'expert',...  43.3 us
    all_to_all x1, waiting for transfers between devices, per_device(): lax.all_to_all(jnp.repeat(packed_grads, shard_count, axis=0), 'expert', s...  42.9 us
    all_to_all x1, waiting for transfers between devices, per_device(): lax.all_to_all(token_piece, 'expert', split_axis=0, concat_axis=0, tiled=...  30 us
    all_to_all x1, starting transfers between devices, per_device(): lax.all_to_all(jnp.repeat(packed_grads, shard_count, axis=0), 'expert', s...  29.5 us
    all_to_all x1, waiting for transfers between devices, per_device(): lax.all_to_all(jnp.repeat(packed_scores, shard_count, axis=0), 'expert',...  20 us
    all_to_all x1, starting transfers between devices, per_device(): lax.all_to_all(score_piece.reshape(expert_count, MOST), 'expert', split_a...  19.2 us
  transfers between devices with their start and end apart: 7, of which 6 were waited for; matrix products, arithmetic and copies ran while one was open for 2% of the time, Pallas kernels for 0%

commit v1 on v0

v1 whole, which is shorter than its diff:
```python
import jax
import jax.numpy as jnp
from jax import lax
from jax.experimental import pallas as pl
from jax.experimental.pallas import tpu as pltpu
from jax.sharding import PartitionSpec as P

MESH = pl.DeviceIdType.MESH
MOST = 8
FOUR = 4
CHUNK = 128
QUARTER = 16
ORDER = (
    *("p1", "l0", "p2", "t1", "l1", "t2", "p3", "l2", "t3"),
    *("a2", "l3", "c2", "a3", "c3", "a1", "c1", "a0", "c0"),
    *("d2", "d3", "f2", "d1", "f3", "g2", "d0", "f1", "g3", "f0", "g1", "g0", "w0"),
)


def flip(v, m):
    hi, lo = v // 2, v % 2
    if m & 2:
        hi = 1 - hi
    if m & 1:
        lo = 1 - lo
    return hi * 2 + lo


def kernel(
    h_tokens, h_grads, route_col, route_row, score_row, h_gate, h_up, h_down,
    out_tokens, out_score, out_gate, out_up, out_down,
    tokens, grads, wpad, wd, xs, xr, disp, own, half, y_s, y_r, z_s, z_r, acts,
    tp, c1_r, c2_s, c2_r, fin, back_r,
    s_in, s_x, r_x, s_st, r_st, s_lo, r_lo, s_y, r_y, s_z, r_z,
    s_ya, r_ya, s_c1, r_c1, s_c2, r_c2, s_b, r_b, known,
):
    f32, bf16 = jnp.float32, jnp.bfloat16
    toks, width = tokens.shape
    hid = wd.shape[1]
    wide = tp.shape[-1]
    lead = width // 128 * 128
    off = width - lead
    e = lax.axis_index("expert")
    f = lax.axis_index("fsdp")
    x, q, p = e // 16, (e // 4) % 4, e % 4
    y, zh, c = f // 4, (f // 2) % 2, f % 2
    inner = (q == 1) | (q == 2)
    middle = (p == 1) | (p == 2)
    group = [q, flip(q, 1), 2 - q // 2, 3 - 3 * (q // 2)]

    def at_x(m):
        return (flip(x, m) * 16 + q * 4 + p, f)

    def at_g(g):
        return (x * 16 + g * 4 + p, f)

    def at_p(m):
        return (x * 16 + q * 4 + flip(p, m), f)

    def at_peer(d, m):
        return (e, flip(y, m) * 4 + zh * 2 + (1 - c if d else c))

    def along_z(step):
        z = (zh * 16 + q * 4 + p + step + 32) % 32
        return (x * 16 + z % 16, y * 4 + (z // 16) * 2 + c)

    at_z = along_z(16)
    peers = [(0, 2), (1, 2), (0, 1), (1, 1), (0, 3), (1, 3), (1, 0)]

    def remote(src, dst, send, recv, to):
        return pltpu.make_async_remote_copy(
            src_ref=src, dst_ref=dst, send_sem=send, recv_sem=recv, device_id=to, device_id_type=MESH
        )

    partners = [at(m) for at in (at_x, at_p) for m in (1, 2, 3)]
    partners += [along_z(4), along_z(-4)] + [at_peer(d, m) for d, m in peers]
    barrier = pltpu.get_barrier_semaphore()
    for to in partners:
        pl.semaphore_signal(barrier, inc=1, device_id=to, device_id_type=MESH)

    loads = [
        pltpu.make_async_copy(src, dst, s_in.at[i])
        for i, (src, dst) in enumerate(
            (
                (h_tokens, tokens),
                (h_grads, grads),
                (h_gate, wpad.at[0, 0:width]),
                (h_up, wpad.at[1, 0:width]),
                (h_down, wd.at[off : off + width]),
            )
        )
    ]
    for copy in loads:
        copy.start()

    col = route_col[...]
    row = route_row[...]
    t_row = lax.broadcasted_iota(jnp.int32, (toks, toks), 0)
    t_col = lax.broadcasted_iota(jnp.int32, (toks, toks), 1)
    same = col == row
    rank_col = jnp.sum(jnp.where(same & (t_col < t_row), 1.0, 0.0), axis=1, keepdims=True)
    rank_row = jnp.sum(jnp.where(same & (t_row < t_col), 1.0, 0.0), axis=0, keepdims=True)

    def expert_of(m):
        xh, xl = x // 2, x % 2
        mh, ml = m // 2, m % 2
        return jnp.where(mh == 1, 1 - xh, xh) * 2 + jnp.where(ml == 1, 1 - xl, xl)

    slot_l = lax.broadcasted_iota(jnp.int32, (toks, 32), 1)
    slot_s = lax.broadcasted_iota(jnp.int32, (32, toks), 0)
    place = jnp.where(
        (col == expert_of(slot_l // MOST)) & (rank_col == (slot_l % MOST).astype(f32)), 1.0, 0.0
    )
    place_t = jnp.where(
        (row == expert_of(slot_s // MOST)) & (rank_row == (slot_s % MOST).astype(f32)), 1.0, 0.0
    )
    packed_s = jnp.sum(place_t * score_row[...], axis=1, keepdims=True)
    blank = jnp.zeros((32, wide - width), f32)
    loads[0].wait()
    loads[1].wait()
    packed_t = jnp.dot(place_t.astype(bf16), tokens[...], preferred_element_type=f32)
    packed_g = jnp.dot(place_t.astype(bf16), grads[...], preferred_element_type=f32)
    packed_t = jnp.concatenate([packed_t, blank], axis=1)
    packed_g = jnp.concatenate([packed_g * packed_s, blank], axis=1)
    for m in range(FOUR):
        xs[m] = jnp.concatenate(
            [packed_t[m * 8 : m * 8 + 8], packed_g[m * 8 : m * 8 + 8]], axis=0
        ).astype(bf16)

    pl.semaphore_wait(barrier, len(partners))

    sent = []

    def go(copy):
        copy.start()
        sent.append(copy)
        return copy

    def go_if(cond, copy):
        pl.when(cond)(copy.start)
        sent.append((cond, copy))

    def tell(hop):
        if hop:
            pl.semaphore_wait(known.at[hop - 1], 1)
        if hop < 3:
            pl.semaphore_signal(
                known.at[hop], inc=1, device_id=along_z(4), device_id_type=MESH
            )

    inx = [go(remote(xs.at[m], xr.at[m], s_x.at[m], r_x.at[m], at_x(m))) for m in (1, 2, 3)]
    tell(0)
    wpad[0, width:wide] = jnp.zeros((wide - width, hid), bf16)
    wpad[1, width:wide] = jnp.zeros((wide - width, hid), bf16)
    wd[0:off] = jnp.zeros((off, hid), bf16)
    for copy in inx:
        copy.wait_recv()
    got = [xs[0].astype(f32)] + [xr[m].astype(f32) for m in (1, 2, 3)]
    rows_t = jnp.concatenate([g[0:8, 0:width] for g in got], axis=0)
    rows_g = jnp.concatenate([g[8:16, 0:width] for g in got], axis=0)
    disp[q, p] = jnp.concatenate([rows_t, rows_g], axis=1).astype(bf16)

    def stride(i, to, n):
        unit = disp.at[group[i], p]
        return remote(unit, unit, s_st.at[i, n], r_st.at[group[i]], at_g(to))

    def local(i, whose, to, n):
        unit = disp.at[group[i], whose]
        return remote(unit, unit, s_lo.at[i, n], r_lo.at[group[i], whose], (x * 16 + q * 4 + to, f))

    def local_sends(i):
        go(local(i, p, flip(p, 1), 0))
        go(local(i, p, 2 - p // 2, 1))

    def relay(i):
        def run():
            for n, whose in enumerate((3 - p, flip(p, 2))):
                local(i, whose, flip(p, 1), 2 + n).wait_recv()
                local(i, whose, flip(p, 1), 2 + n).start()

        pl.when(middle)(run)
        for n, whose in enumerate((3 - p, flip(p, 2))):
            sent.append((middle, local(i, whose, flip(p, 1), 2 + n)))

    outer, mate = flip(q, 1), 3 - q
    go(stride(0, outer, 0))
    go_if(inner, stride(0, mate, 1))
    local_sends(0)

    def pass_on(i):
        stride(i, outer, 0).wait_recv()
        go_if(inner, stride(i, mate if i == 1 else outer, 0))
        local_sends(i)

    y_sum = [None] * 4
    z_sum = [None] * 4
    c1 = [None] * 4

    def stage_a(i):
        g = group[i]
        local(i, flip(p, 1), flip(p, 1), 0).wait_recv()

        @pl.when(jnp.logical_not(middle))
        def _():
            for whose in (3 - p, flip(p, 2)):
                local(i, whose, flip(p, 1), 0).wait_recv()

        unit = disp[g].reshape(CHUNK, 2 * width)
        t, u = unit[:, 0:width], unit[:, lead:]
        weights = ((t, wpad[0, 0:width]), (t, wpad[1, 0:width]), (u, wd[...]))
        for n, (rows, weight) in enumerate(weights):
            v = jnp.dot(rows, weight, preferred_element_type=f32)
            v = v.reshape(2, 4, QUARTER, hid)
            own[:, :, :, n * hid : (n + 1) * hid] = v
            y_s[i, :, :, :, n * hid : (n + 1) * hid] = v.astype(bf16)
        y_sum[i] = []
        for d, m in peers:
            block = y_s.at[i, 1 - c if d else c, flip(y, m)]
            k = d * 4 + m
            y_sum[i].append(go(remote(block, y_r.at[i, k], s_y.at[i, k], r_y.at[i, k], at_peer(d, m))))
        half[i] = own[c, y]

    def stage_c(i):
        for copy in y_sum[i]:
            copy.wait_recv()
        v = half[i]
        for d, m in peers:
            v = v + y_r[i, d * 4 + m].astype(f32)
        half[i] = v
        z_s[i] = v.astype(bf16)
        z_sum[i] = go(remote(z_s.at[i], z_r.at[i], s_z.at[i], r_z.at[i], at_z))

    def stage_d(i):
        z_sum[i].wait_recv()
        v = half[i] + z_r[i].astype(f32)
        gate, up, back = v[:, 0:hid], v[:, hid : 2 * hid], v[:, 2 * hid : 3 * hid]
        sig = jax.nn.sigmoid(gate)
        silu = gate * sig
        hidden = silu * up
        acts[i, c, y, :, 0:hid] = (back * up * sig * (1.0 + gate * (1.0 - sig))).astype(bf16)
        acts[i, c, y, :, hid : 2 * hid] = (back * silu).astype(bf16)
        acts[i, c, y, :, 2 * hid : 3 * hid] = hidden.astype(bf16)
        piece = jnp.sum(hidden * back, axis=1, keepdims=True)
        acts[i, c, y, :, 3 * hid : 3 * hid + 128] = jnp.broadcast_to(piece, (QUARTER, 128)).astype(bf16)
        mine = acts.at[i, c, y]
        for d, m in peers:
            k = d * 4 + m
            go(remote(mine, mine, s_ya.at[i, k], r_ya.at[i, k], at_peer(d, m)))

    def stage_f(i):
        for d, m in peers:
            k = d * 4 + m
            theirs = acts.at[i, 1 - c if d else c, flip(y, m)]
            remote(theirs, theirs, s_ya.at[i, k], r_ya.at[i, k], at_peer(d, m)).wait_recv()
        a = acts[i].reshape(CHUNK, acts.shape[-1])
        nt = (((1,), (1,)), ((), ()))
        v = lax.dot_general(a[:, 0:hid], wpad[0], nt, preferred_element_type=f32)
        v = v + lax.dot_general(a[:, hid : 2 * hid], wpad[1], nt, preferred_element_type=f32)
        piece = a[:, 3 * hid : 3 * hid + 1].astype(f32)
        at = lax.broadcasted_iota(jnp.int32, (CHUNK, wide), 1)
        v = jnp.where(at == width, piece, v)
        tp[i] = v.astype(bf16).reshape(4, 32, wide)
        c1[i] = [
            go(remote(tp.at[i, flip(p, m)], c1_r.at[i, m], s_c1.at[i, m], r_c1.at[i, m], at_p(m)))
            for m in (1, 2, 3)
        ]

    def stage_g(i):
        for copy in c1[i]:
            copy.wait_recv()
        v = tp[i, p].astype(f32)
        for m in (1, 2, 3):
            v = v + c1_r[i, m].astype(f32)
        if i == 0:
            fin[...] = v
        else:
            c2_s[i] = v.astype(bf16)
            go(remote(c2_s.at[i], c2_r.at[q], s_c2.at[i], r_c2.at[q], at_g(group[i])))

    def stage_w(_):
        a = acts[...].reshape(4, CHUNK, acts.shape[-1])
        tn = (((0,), (0,)), ((), ()))
        units = jnp.concatenate([disp[g].reshape(CHUNK, 2 * width) for g in group], axis=0)
        ts, gs = units[:, 0:width], units[:, lead:]
        a = a.reshape(4 * CHUNK, acts.shape[-1])
        out_gate[...] = lax.dot_general(ts, a[:, 0:hid], tn, preferred_element_type=f32).astype(bf16)
        out_up[...] = lax.dot_general(ts, a[:, hid : 2 * hid], tn, preferred_element_type=f32).astype(bf16)
        v = lax.dot_general(gs, a[:, 2 * hid : 3 * hid], tn, preferred_element_type=f32)
        out_down[...] = v[off:].astype(bf16)

    stages = {"p": pass_on, "t": tell, "l": relay, "a": stage_a, "c": stage_c, "d": stage_d}
    stages.update({"f": stage_f, "g": stage_g, "w": stage_w})
    loads[2].wait()
    loads[3].wait()
    loads[4].wait()
    for step in ORDER:
        stages[step[0]](int(step[1]))

    for i in (1, 2, 3):
        part = c2_r.at[group[i]]
        remote(part, part, s_c2.at[i], r_c2.at[group[i]], at_g(group[i])).wait_recv()
    v = fin[...]
    for i in (1, 2, 3):
        v = v + c2_r[group[i]].astype(f32)
    fin[...] = v
    back = [
        go(remote(fin.at[pl.ds(m * 8, 8)], back_r.at[m], s_b.at[m], r_b.at[m], at_x(m)))
        for m in (1, 2, 3)
    ]

    for copy in back:
        copy.wait_recv()
    v = jnp.concatenate([fin[0:8]] + [back_r[m] for m in (1, 2, 3)], axis=0)
    total = jnp.sum(place_t * v[:, width : width + 1], axis=0, keepdims=True)
    out_score[...] = total / score_row[...]
    v = jnp.dot(place.astype(bf16), v[:, 0:width].astype(bf16), preferred_element_type=f32)
    out_tokens[...] = v.astype(bf16)

    for item in sent:
        if isinstance(item, tuple):
            pl.when(item[0])(item[1].wait_send)
        else:
            item.wait_send()


def per_device(tokens, route, score, grad_out, w_gate, w_up, w_down):
    toks, width = tokens.shape
    hid = w_gate.shape[1]
    wide = -(-width // 128) * 128
    bf16, f32 = jnp.bfloat16, jnp.float32
    vm = pltpu.VMEM
    dma = pltpu.SemaphoreType.DMA
    scratch = [
        vm((toks, width), bf16),
        vm((toks, width), bf16),
        vm((2, wide, hid), bf16),
        vm((wide, hid), bf16),
        vm((4, 16, wide), bf16),
        vm((4, 16, wide), bf16),
        vm((4, 4, 32, 2 * width), bf16),
        vm((2, 4, QUARTER, 3 * hid), f32),
        vm((4, QUARTER, 3 * hid), f32),
        vm((4, 2, 4, QUARTER, 3 * hid), bf16),
        vm((4, 8, QUARTER, 3 * hid), bf16),
        vm((4, QUARTER, 3 * hid), bf16),
        vm((4, QUARTER, 3 * hid), bf16),
        vm((4, 2, 4, QUARTER, 3 * hid + 128), bf16),
        vm((4, 4, 32, wide), bf16),
        vm((4, 4, 32, wide), bf16),
        vm((4, 32, wide), bf16),
        vm((4, 32, wide), bf16),
        vm((32, wide), f32),
        vm((4, 8, wide), f32),
    ]
    shapes = [(5,)]
    shapes += [(4,), (4,), (4, 2), (4,), (4, 4), (4, 4)]
    shapes += [(4, 8), (4, 8), (4,), (4,)]
    shapes += [(4, 8), (4, 8)]
    shapes += [(4, 4), (4, 4), (4,), (4,), (4,), (4,)]
    scratch += [dma(shape) for shape in shapes]
    scratch.append(pltpu.SemaphoreType.REGULAR((3,)))
    outs = pl.pallas_call(
        kernel,
        out_shape=(
            jax.ShapeDtypeStruct((toks, width), bf16),
            jax.ShapeDtypeStruct((1, toks), f32),
            jax.ShapeDtypeStruct((width, hid), bf16),
            jax.ShapeDtypeStruct((width, hid), bf16),
            jax.ShapeDtypeStruct((width, hid), bf16),
        ),
        in_specs=[pl.BlockSpec(memory_space=pltpu.HBM if i in (0, 1, 5, 6, 7) else vm) for i in range(8)],
        out_specs=(pl.BlockSpec(memory_space=vm),) * 5,
        scratch_shapes=scratch,
        compiler_params=pltpu.CompilerParams(
            collective_id=0, has_side_effects=True, vmem_limit_bytes=60 << 20
        ),
        cost_estimate=pl.CostEstimate(
            flops=16 * 512 * width * hid, bytes_accessed=12 * width * hid, transcendentals=64 * hid
        ),
    )(
        tokens,
        grad_out,
        route,
        route.reshape(1, toks),
        score.astype(f32).reshape(1, toks),
        w_gate,
        w_up,
        w_down.T,
    )
    grad_tokens, grad_score, grad_gate, grad_up, grad_down = outs
    return (grad_tokens, grad_score.reshape(toks), grad_gate, grad_up, grad_down.T)


def solution(mesh):
    return jax.shard_map(
        per_device,
        mesh=mesh,
        in_specs=(
            P("expert", "fsdp"),
            P("expert", None),
            P("expert"),
            P("expert", "fsdp"),
            P("fsdp", "expert"),
            P("fsdp", "expert"),
            P("expert", "fsdp"),
        ),
        out_specs=(
            P("expert", "fsdp"),
            P("expert"),
            P("fsdp", "expert"),
            P("fsdp", "expert"),
            P("expert", "fsdp"),
        ),
        check_vma=False,
    )
```

time: 562 us -> 130 us (0.23)
  waiting for transfers between devices: 329 us -> 0 us
  Pallas kernels: 0 us -> 121 us
  blocking collectives: 112 us -> 0 us
  starting transfers between devices: 82.5 us -> 0 us
  between operations: 14.9 us -> 0.66 us
  matrix products: 10.7 us -> 0 us
    reduce_scatter x1 -> x0, waiting for transfers between devices: 177 us -> none  [per_device(): lax.psum_scatter(jnp.concatenate([forward, backward], axis=1), 'fsdp', sc...]
    all_to_all x5 -> x0, waiting for transfers between devices: 152 us -> none  [the longest x1 43.3 us: per_device(): lax.all_to_all(jnp.repeat(packed_tokens, shard_count, axis=0), 'expert',...]
    pallas_call x0 -> x1, Pallas kernels: none -> 121 us  [per_device(): pl.pallas_call(kernel, out_shape=(jax.ShapeDtypeStruct((toks, width), bf1...]
    unnamed x1 -> x0, blocking collectives: 112 us -> none
    all_to_all x5 -> x0, starting transfers between devices: 82.4 us -> none  [the longest x1 29.5 us: per_device(): lax.all_to_all(jnp.repeat(packed_grads, shard_count, axis=0), 'expert', s...]
    dot_general x12 -> x0, matrix products: 10.7 us -> none  [the longest x1 1.53 us: per_device(): lax.dot_general(up_grad, w_up, contract_cols, preferred_element_type=jnp....]
  transfers between devices with their start and end apart: 7 -> 0, of which waited for: 6 -> 0; matrix products, arithmetic and copies ran while one was open for 2% -> 0% of each run, Pallas kernels for 0% -> 0%
where the time goes in v1:
time: 130 us; the launch traced here: 129 us
  Pallas kernels  121 us (93%)
  local copies, waits for them, and re-layouts  6.9 us (5%)
    pallas_call x1, Pallas kernels, per_device(): pl.pallas_call(kernel, out_shape=(jax.ShapeDtypeStruct((toks, width), bf1...  121 us
    unnamed x16, local copies, waits for them, and re-layouts  6.9 us

profile of v1, /device:TPU:6, one launch (start us, length us, event | category | flops | bytes accessed | tf_op | source)
XLA Modules:
  0.0 128.8 jit_solution(15693785097864769112)
XLA Ops:
  0.6 0.0 copy-start.3
  0.6 0.6 copy-done.3
  1.3 0.0 copy-start.2
  1.3 0.5 bitcast_convert_fusion.score_row
  1.8 0.1 copy-done.2
  1.9 0.7 copy.12.route_col
  2.6 120.8 %shard_map.110 = (bf16[24,320]{1,0:T(8,128)(2,1)}, f32[1,24]{1,0:T(1,128)}, bf16[320,512]{1,0:T(8,128)(2,1)}, bf16[320,512]{1,0:T(8,128)(2,1)}, bf16[320,512]{1,0:T(8,128)(2,1)}) custom-call(bf16[24,320]{1,0:T(8,128)(2,1)} %h_tokens.1, bf16[24,320]{1,0:T(8,128)(2,1)} %h_grads.1, s32[24,1]{1,0:T(8,128)} %copy.12.route_col, s32[1,24]{1,0:T(1,128)} %bitcast.8, ...), custom_call_target="tpu_custom_call" | custom-call | flops 1342177280 | bytes 1966080 | tf_op jit(solution)/shard_map/pallas_call | solution.py:362
  123.4 0.0 copy-start.4
  123.4 1.3 %copy.18 = bf16[24,320]{1,0:T(8,128)(2,1)} copy(bf16[24,320]{1,0:T(8,128)(2,1)} %get-tuple-element.20) | data formatting | bytes 30720
  124.7 0.0 copy-done.4
  124.7 0.5 copy.19
  125.2 0.0 copy-start.1
  125.3 1.8 %copy.20 = bf16[320,512]{1,0:T(8,128)(2,1)} copy(bf16[320,512]{1,0:T(8,128)(2,1)} %get-tuple-element.22) | data formatting | bytes 655360
  127.0 0.0 copy-done.1
  127.0 0.0 copy-start
  127.0 0.7 copy.21
  127.7 0.4 copy-done
  128.1 0.7 copy.22
Async XLA Ops:
  0.6 0.7 copy-start.3
  1.3 0.7 copy-start.2
  123.4 1.3 %copy-start.4 = (f32[1,24]{1,0:T(1,128)S(1)}, f32[1,24]{1,0:T(1,128)}, u32[]{:S(2)}) copy-start(f32[1,24]{1,0:T(1,128)} %get-tuple-element.11) | copy-start | bytes 292
  125.2 1.8 %copy-start.1 = (bf16[320,512]{1,0:T(8,128)(2,1)S(1)}, bf16[320,512]{1,0:T(8,128)(2,1)}, u32[]{:S(2)}) copy-start(bf16[320,512]{1,0:T(8,128)(2,1)} %get-tuple-element.23) | copy-start | bytes 983044
  127.0 1.1 copy-start
